TPU v7x, 32 devices: a whole 2x2x4 slice. The times are simulated.
32 devices in a mesh: groups: 2 (over y), row: 4 (over z), col: 4 (over x, core).
Axes of the slice: x: 2, y: 2, z: 4, core: 2. Of those that a mesh axis runs over, the one named last changes fastest.
Arguments:
- grads_now: float32 [3072, 8192], P(('groups', 'col'), 'row'), parts along dimension 0, as said below
- grads_later: float32 [3072, 8192], P(('groups', 'row'), 'col'), parts along dimension 0, as said below
Outputs:
- covariance: float32 [16384, 8192], P(('groups', 'row'), 'col'), parts along dimension 0
There are 2 independent parts, one for each index of `groups`. A program takes and returns all parts, laid end to end along the dimension named above; each array names one. Nothing has to cross between parts.
Inputs may be any that keep to these rules, and one draw needn't show every extreme that they name: `grads_now`: gradients of two checkpoints of one model; per-feature scales differ. `grads_later`: gradients at the later checkpoint, correlated with those at checkpoint t.
All inputs are finite; a program needn't handle non-finite values.
Results may differ from a plain program's by a relative error of at most 0.00015.
Values sent between devices are 32-bit elements; how exact they have to be, the bound alone decides.
A program may use at most 128 MiB of HBM per device.

v0:
```python
import jax
import jax.numpy as jnp
from jax import lax
from jax.sharding import PartitionSpec as P


def contract(left, right):
    return lax.dot_general(
        left,
        right,
        (((0,), (0,)), ((), ())),
        precision=lax.Precision.HIGHEST,
        preferred_element_type=jnp.float32,
    )


def on_device(grads_now, grads_later):
    all_now = lax.all_gather(grads_now, "col", axis=0, tiled=True)
    count = all_now.shape[0]
    centered = all_now - jnp.mean(all_now, axis=0, keepdims=True)
    product = contract(centered, lax.all_gather(grads_later, "row", axis=0, tiled=True))
    return product / jnp.float32(count - 1)


def solution(mesh):
    placed = (P(("groups", "col"), "row"), P(("groups", "row"), "col"))
    return jax.shard_map(
        on_device,
        mesh=mesh,
        in_specs=placed,
        out_specs=P(("groups", "row"), "col"),
        check_vma=False,
    )
```

profile of v0, /device:TPU:0, one launch (start us, length us, event | category | flops | bytes accessed | tf_op | source)
XLA Modules:
  0.0 407.3 jit_solution(16542437366660550539)
XLA Ops:
  6.5 0.0 all-gather.3.cloned.1.call-start
  6.5 0.7 all-gather.3.cloned.1.call-update
  7.3 0.0 all-gather.5.cloned.1.call-start
  7.3 0.7 all-gather.5.cloned.1.call-update
  8.0 85.7 %all-gather.3.cloned.1.call-done = f32[1536,2048]{1,0:T(8,128)} async-done(((f32[384,2048]{1,0:T(8,128)}), f32[1536,2048]{1,0:T(8,128)}) %all-gather.3.cloned.1.call-update) | async-done | bytes 12582928 | tf_op jit(solution)/shard_map/all_gather | solution.py:18
  93.8 5.2 %reduce_sum.9 = f32[2048]{0:T(1024)S(1)} reduce(f32[1536,2048]{1,0:T(8,128)} %all-gather.3.cloned.1.call-done, f32[]{:T(128)} %constant.2.clone.1), dimensions={0}, to_apply=%region_0.0 | reduce | flops 3143680 | bytes 12591108 | tf_op jit(solution)/shard_map/reduce_sum | solution.py:20
  99.0 214.6 %all-gather.5.cloned.1.call-done = f32[1536,2048]{1,0:T(8,128)} async-done(((f32[384,2048]{1,0:T(8,128)}), f32[1536,2048]{1,0:T(8,128)}) %all-gather.5.cloned.1.call-update) | async-done | bytes 12582928 | tf_op jit(solution)/shard_map/all_gather | solution.py:21
  313.6 86.9 %fusion.2 = f32[2048,2048]{1,0:T(8,128)} fusion(f32[1536,2048]{1,0:T(8,128)} %all-gather.5.cloned.1.call-done, f32[1536,2048]{1,0:T(8,128)} %all-gather.3.cloned.1.call-done, f32[2048]{0:T(1024)S(1)} %broadcast_multiply_fusion), kind=kOutput, calls=%fused_computation.2 | convolution fusion | flops 77316751360 | bytes 41951232 | tf_op jit(solution)/shard_map/dot_general | solution.py:8
  (1 shorter events, 0.0 us)
Async XLA Ops:
  6.5 87.2 %all-gather.3.cloned.1.call-start = ((), (), s32[]{:S(2)}) async-start(), calls=%async_computation | async-start | bytes 15728640 | tf_op jit(solution)/shard_map/all_gather | solution.py:18
  7.3 306.3 %all-gather.5.cloned.1.call-start = ((), (), s32[]{:S(2)}) async-start(), calls=%async_computation.1 | async-start | bytes 15728640 | tf_op jit(solution)/shard_map/all_gather | solution.py:21
Sparse Core Ops, SparseCore 0:
  8.9 84.7 all-gather.2
  95.3 218.2 all-gather.4
where the time goes:
time: 407 us
  waiting for transfers between devices  302 us (74%)
  matrix products  86.9 us (21%)
  between operations  13.4 us (3%)
  other arithmetic  5.23 us (1%)
    all_gather x1, waiting for transfers between devices, on_device(): lax.all_gather(grads_later, 'row', axis=0, tiled=True)  215 us
    dot_general x1, matrix products, contract(): lax.dot_general(left, right, (((0,), (0,)), ((), ())), precision=lax.Prec...  86.9 us
    all_gather x1, waiting for transfers between devices, on_device(): all_now = lax.all_gather(grads_now, 'col', axis=0, tiled=True)  85.7 us
  transfers between devices with their start and end apart: 2, of which 2 were waited for; matrix products, arithmetic and copies ran while one was open for 1% of the time, Pallas kernels for 0%

commit v1 on v0

v1 whole, which is shorter than its diff:
```python
import functools

import jax
import jax.numpy as jnp
from jax import lax
from jax.experimental import pallas as pl
from jax.experimental.pallas import tpu as pltpu
from jax.sharding import PartitionSpec as P

MESH = pl.DeviceIdType.MESH
CHUNKS = 4
TILE = 256


def contract(left, right):
    return lax.dot_general(
        left,
        right,
        (((0,), (0,)), ((), ())),
        precision=lax.Precision.HIGHEST,
        preferred_element_type=jnp.float32,
    )


def split(x):
    high = x.astype(jnp.bfloat16)
    low = (x - high.astype(jnp.float32)).astype(jnp.bfloat16)
    return high, low


def kernel(
    n, now_ref, later_ref, out_ref,
    acc, lhs, rhs, held,
    own_now, own_later, now_send, now_recv, z_send, z_recv, out_sem,
):
    r, c = lax.axis_index("row"), lax.axis_index("col")
    rows, feats = now_ref.shape
    cols = later_ref.shape[1]
    width = cols // CHUNKS
    piece = rows // CHUNKS
    count = 4 * rows
    partner = c + 1 - 2 * (c % 2)
    across = (c + 2) % 4
    last = lax.max(r, n - 1 - r)

    def slot(block, ch):
        start = pl.multiple_of(block * rows + ch * piece, piece)
        return acc.at[pl.ds(start, piece), :]

    def columns(ch):
        return pl.ds(pl.multiple_of(ch * width, width), width)

    def now_copy(kind, ch, src, block, target):
        return pltpu.make_async_remote_copy(
            src_ref=src,
            dst_ref=slot(block, ch),
            send_sem=now_send.at[kind, ch],
            recv_sem=now_recv.at[kind, ch],
            device_id={"col": target},
            device_id_type=MESH,
        )

    def own_piece(ch):
        return now_ref.at[pl.ds(pl.multiple_of(ch * piece, piece), piece), :]

    def line_copy(side, origin, ch, src, target):
        return pltpu.make_async_remote_copy(
            src_ref=src,
            dst_ref=held.at[origin, ch],
            send_sem=z_send.at[side, origin, ch],
            recv_sem=z_recv.at[origin, ch],
            device_id={"row": target},
            device_id_type=MESH,
        )

    def in_line(i):
        return (i >= 0) & (i < n)

    def own_later_copy(ch):
        return pltpu.make_async_copy(later_ref.at[:, columns(ch)], held.at[r, ch], own_later.at[ch])

    def out_copy(ch):
        return pltpu.make_async_copy(acc.at[:, columns(ch)], out_ref.at[:, columns(ch)], out_sem.at[ch])

    barrier = pltpu.get_barrier_semaphore()
    pl.semaphore_signal(barrier, inc=1, device_id={"col": partner}, device_id_type=MESH)
    pl.semaphore_signal(barrier, inc=1, device_id={"col": across}, device_id_type=MESH)
    for side in range(2):
        target = r - 1 + 2 * side

        @pl.when(in_line(target))
        def _():
            pl.semaphore_signal(barrier, inc=1, device_id={"row": target}, device_id_type=MESH)

    pl.semaphore_wait(barrier, 2 + (r > 0).astype(jnp.int32) + (r < n - 1).astype(jnp.int32))

    def start_own(ch, carry):
        for side in range(2):
            target = r - 1 + 2 * side

            @pl.when(in_line(target))
            def _():
                line_copy(side, r, ch, later_ref.at[:, columns(ch)], target).start()

        now_copy(1, ch, own_piece(ch), c, across).start()
        now_copy(0, ch, own_piece(ch), c, partner).start()
        own_later_copy(ch).start()
        return carry

    lax.fori_loop(0, CHUNKS, start_own, 0)
    own_start = pl.multiple_of(c * rows, rows)
    copy_now = pltpu.make_async_copy(now_ref, acc.at[pl.ds(own_start, rows), :], own_now)
    copy_now.start()

    def relay(d, ch, side):
        origin = r + d * (1 - 2 * side)
        target = r - 1 + 2 * side

        @pl.when(in_line(origin))
        def _():
            line_copy(side, origin, ch, held.at[origin, ch], target).wait_recv()

            @pl.when(in_line(target))
            def _():
                line_copy(side, origin, ch, held.at[origin, ch], target).start()

    def first(ch, carry):
        now_copy(1, ch, own_piece(ch), across, across).wait_recv()
        now_copy(2, ch, slot(across, ch), across, partner).start()
        relay(1, ch, 0)
        relay(1, ch, 1)
        return carry

    lax.fori_loop(0, CHUNKS, first, 0)

    def settle(ch, carry):
        now_copy(0, ch, own_piece(ch), partner, partner).wait_recv()
        now_copy(2, ch, slot(across, ch), (partner + 2) % 4, partner).wait_recv()
        now_copy(2, ch, slot(across, ch), across, partner).wait_send()
        return carry

    lax.fori_loop(0, CHUNKS, settle, 0)
    copy_now.wait()

    def center(j, carry):
        at = pl.ds(pl.multiple_of(j * TILE, TILE), TILE)
        total = jnp.sum(acc[pl.ds(0, count), at], axis=0, keepdims=True)
        mean = total / jnp.float32(count)
        for block in range(4):
            part = (acc[pl.ds(block * rows, rows), at] - mean) / jnp.float32(count - 1)
            high, low = split(part.T)
            lhs[block, at, pl.ds(0, rows)] = high
            lhs[block, at, pl.ds(rows, rows)] = low
            lhs[block, at, pl.ds(2 * rows, rows)] = high
        return carry

    lax.fori_loop(0, feats // TILE, center, 0)

    def clear(j, carry):
        at = pl.ds(pl.multiple_of(j * TILE, TILE), TILE)
        acc[at, :] = jnp.zeros((TILE, cols), jnp.float32)
        return carry

    lax.fori_loop(0, feats // TILE, clear, 0)

    def multiply(origin, ch):
        high, low = split(held[origin, ch])
        rhs[pl.ds(0, rows), :] = high
        rhs[pl.ds(rows, rows), :] = high
        rhs[pl.ds(2 * rows, rows), :] = low

        def tile(i, carry):
            at = pl.ds(pl.multiple_of(i * TILE, TILE), TILE)
            acc[at, columns(ch)] += jnp.dot(
                lhs[origin, at, :], rhs[...], preferred_element_type=jnp.float32
            )
            return carry

        lax.fori_loop(0, feats // TILE, tile, 0)

    def step(t, carry):
        d, ch = t // CHUNKS, t % CHUNKS

        def one_side(side, inner):
            origin = r + d * (1 - 2 * side)

            @pl.when(in_line(origin) & (d + 1 - side > 0))
            def _():
                @pl.when(d == 0)
                def _():
                    own_later_copy(ch).wait()

                @pl.when(d >= 2)
                def _():
                    relay(d, ch, side)

                multiply(origin, ch)

            return inner

        lax.fori_loop(0, 2, one_side, 0)

        @pl.when(d == last)
        def _():
            out_copy(ch).start()

        return carry

    lax.fori_loop(0, n * CHUNKS, step, 0)

    def finish(ch, carry):
        now_copy(0, ch, own_piece(ch), c, partner).wait_send()
        now_copy(1, ch, own_piece(ch), c, across).wait_send()
        for side in range(2):
            target = r - 1 + 2 * side
            for d in range(n):
                origin = r + d * (1 - 2 * side)

                @pl.when(in_line(origin) & in_line(target))
                def _():
                    line_copy(side, origin, ch, held.at[origin, ch], target).wait_send()

        out_copy(ch).wait()
        return carry

    lax.fori_loop(0, CHUNKS, finish, 0)


def fused(n, grads_now, grads_later):
    rows, feats = grads_now.shape
    cols = grads_later.shape[1]
    return pl.pallas_call(
        functools.partial(kernel, n),
        out_shape=jax.ShapeDtypeStruct((feats, cols), jnp.float32),
        in_specs=[pl.BlockSpec(memory_space=pl.ANY)] * 2,
        out_specs=pl.BlockSpec(memory_space=pl.ANY),
        scratch_shapes=[
            pltpu.VMEM((feats, cols), jnp.float32),
            pltpu.VMEM((4, feats, 3 * rows), jnp.bfloat16),
            pltpu.VMEM((3 * rows, cols // CHUNKS), jnp.bfloat16),
            pltpu.VMEM((n, CHUNKS, rows, cols // CHUNKS), jnp.float32),
            pltpu.SemaphoreType.DMA,
            pltpu.SemaphoreType.DMA((CHUNKS,)),
            pltpu.SemaphoreType.DMA((3, CHUNKS)),
            pltpu.SemaphoreType.DMA((3, CHUNKS)),
            pltpu.SemaphoreType.DMA((2, n, CHUNKS)),
            pltpu.SemaphoreType.DMA((n, CHUNKS)),
            pltpu.SemaphoreType.DMA((CHUNKS,)),
        ],
        compiler_params=pltpu.CompilerParams(
            collective_id=0, has_side_effects=True, vmem_limit_bytes=58 * 2**20
        ),
        cost_estimate=pl.CostEstimate(
            flops=6 * n * rows * feats * cols,
            bytes_accessed=4 * (feats * cols + 2 * n * rows * cols),
            transcendentals=0,
        ),
    )(grads_now, grads_later)


def gathered(grads_now, grads_later):
    all_now = lax.all_gather(grads_now, "col", axis=0, tiled=True)
    count = all_now.shape[0]
    centered = all_now - jnp.mean(all_now, axis=0, keepdims=True)
    product = contract(centered, lax.all_gather(grads_later, "row", axis=0, tiled=True))
    return product / jnp.float32(count - 1)


def on_device(shape, grads_now, grads_later):
    n = shape["row"]
    rows, feats = grads_now.shape
    cols = grads_later.shape[1]
    fits = (
        shape["col"] == 4
        and n == 4
        and grads_later.shape[0] == rows
        and rows % (32 * CHUNKS) == 0
        and feats % TILE == 0
        and cols % (128 * CHUNKS) == 0
        and 4 * rows <= feats
        and feats == cols
    )
    if fits:
        return fused(n, grads_now, grads_later)
    return gathered(grads_now, grads_later)


def solution(mesh):
    placed = (P(("groups", "col"), "row"), P(("groups", "row"), "col"))
    return jax.shard_map(
        functools.partial(on_device, dict(mesh.shape)),
        mesh=mesh,
        in_specs=placed,
        out_specs=P(("groups", "row"), "col"),
        check_vma=False,
    )
```

time: 407 us -> 226 us (0.56)
  waiting for transfers between devices: 302 us -> 0 us
  Pallas kernels: 0 us -> 214 us
  matrix products: 86.9 us -> 0 us
  between operations: 13.4 us -> 0.01 us
  local copies, waits for them, and re-layouts: 0 us -> 11.8 us
  other arithmetic: 5.23 us -> 0 us
    all_gather x2 -> x0, waiting for transfers between devices: 300 us -> none  [the longest x1 215 us: on_device(): lax.all_gather(grads_later, 'row', axis=0, tiled=True)]
    pallas_call x0 -> x1, Pallas kernels: none -> 214 us  [fused(): pl.pallas_call(functools.partial(kernel, n), out_shape=jax.ShapeDtypeStru...]
    dot_general x1 -> x0, matrix products: 86.9 us -> none  [contract(): lax.dot_general(left, right, (((0,), (0,)), ((), ())), precision=lax.Prec...]
    unnamed x0 -> x1, local copies, waits for them, and re-layouts: none -> 11.8 us
    reduce_sum x1 -> x0, other arithmetic: 5.22 us -> none  [on_device(): centered = all_now - jnp.mean(all_now, axis=0, keepdims=True)]
  transfers between devices with their start and end apart: 2 -> 0, of which waited for: 2 -> 0; matrix products, arithmetic and copies ran while one was open for 1% -> 0% of each run, Pallas kernels for 0% -> 0%
where the time goes in v1:
time: 226 us
  Pallas kernels  214 us (95%)
  local copies, waits for them, and re-layouts  11.8 us (5%)
    pallas_call x1, Pallas kernels, fused(): pl.pallas_call(functools.partial(kernel, n), out_shape=jax.ShapeDtypeStru...  214 us
    unnamed x1, local copies, waits for them, and re-layouts  11.8 us

profile of v1, /device:TPU:0, one launch (start us, length us, event | category | flops | bytes accessed | tf_op | source)
XLA Modules:
  0.0 226.1 jit_solution(15300478608760746063)
XLA Ops:
  0.0 214.3 %shard_map.28 = f32[2048,2048]{1,0:T(8,128)} custom-call(f32[384,2048]{1,0:T(8,128)} %now_ref.1, f32[384,2048]{1,0:T(8,128)} %later_ref.1), custom_call_target="tpu_custom_call" | custom-call | flops 38654705664 | bytes 41943040 | tf_op jit(solution)/shard_map/pallas_call | solution.py:232
  214.3 11.8 %copy.4 = f32[2048,2048]{1,0:T(8,128)} copy(f32[2048,2048]{1,0:T(8,128)} %shard_map.28) | data formatting | bytes 33554432

commit v2 on v1

--- a/solution.py
+++ b/solution.py
@@ -9,6 +9,9 @@
 
 MESH = pl.DeviceIdType.MESH
 CHUNKS = 4
+FIRST_MIB = 34
+LAST_MIB = 10
+TAIL = 1
 TILE = 256
 
 
@@ -29,9 +32,9 @@
 
 
 def kernel(
-    n, now_ref, later_ref, out_ref,
-    acc, lhs, rhs, held,
-    own_now, own_later, now_send, now_recv, z_send, z_recv, out_sem,
+    n, now_ref, later_ref, acc, lhs_last, rhs_last,
+    lhs, rhs, held,
+    own_now, own_later, now_send, now_recv, z_send, z_recv,
 ):
     r, c = lax.axis_index("row"), lax.axis_index("col")
     rows, feats = now_ref.shape
@@ -41,7 +44,6 @@
     count = 4 * rows
     partner = c + 1 - 2 * (c % 2)
     across = (c + 2) % 4
-    last = lax.max(r, n - 1 - r)
 
     def slot(block, ch):
         start = pl.multiple_of(block * rows + ch * piece, piece)
@@ -78,9 +80,6 @@
 
     def own_later_copy(ch):
         return pltpu.make_async_copy(later_ref.at[:, columns(ch)], held.at[r, ch], own_later.at[ch])
-
-    def out_copy(ch):
-        return pltpu.make_async_copy(acc.at[:, columns(ch)], out_ref.at[:, columns(ch)], out_sem.at[ch])
 
     barrier = pltpu.get_barrier_semaphore()
     pl.semaphore_signal(barrier, inc=1, device_id={"col": partner}, device_id_type=MESH)
@@ -152,6 +151,13 @@
             lhs[block, at, pl.ds(0, rows)] = high
             lhs[block, at, pl.ds(rows, rows)] = low
             lhs[block, at, pl.ds(2 * rows, rows)] = high
+
+            @pl.when(block == n - 1 - r)
+            def _():
+                lhs_last[at, pl.ds(0, rows)] = high
+                lhs_last[at, pl.ds(rows, rows)] = low
+                lhs_last[at, pl.ds(2 * rows, rows)] = high
+
         return carry
 
     lax.fori_loop(0, feats // TILE, center, 0)
@@ -163,11 +169,14 @@
 
     lax.fori_loop(0, feats // TILE, clear, 0)
 
+    def place(to, origin, ch):
+        high, low = split(held[origin, ch])
+        to[pl.ds(0, rows), :] = high
+        to[pl.ds(rows, rows), :] = high
+        to[pl.ds(2 * rows, rows), :] = low
+
     def multiply(origin, ch):
-        high, low = split(held[origin, ch])
-        rhs[pl.ds(0, rows), :] = high
-        rhs[pl.ds(rows, rows), :] = high
-        rhs[pl.ds(2 * rows, rows), :] = low
+        place(rhs, origin, ch)
 
         def tile(i, carry):
             at = pl.ds(pl.multiple_of(i * TILE, TILE), TILE)
@@ -194,15 +203,17 @@
                 def _():
                     relay(d, ch, side)
 
-                multiply(origin, ch)
+                @pl.when(t < n * CHUNKS - TAIL)
+                def _():
+                    multiply(origin, ch)
+
+                @pl.when(t >= n * CHUNKS - TAIL)
+                def _():
+                    place(rhs_last.at[t - (n * CHUNKS - TAIL)], origin, ch)
 
             return inner
 
         lax.fori_loop(0, 2, one_side, 0)
-
-        @pl.when(d == last)
-        def _():
-            out_copy(ch).start()
 
         return carry
 
@@ -220,22 +231,79 @@
                 def _():
                     line_copy(side, origin, ch, held.at[origin, ch], target).wait_send()
 
-        out_copy(ch).wait()
         return carry
 
     lax.fori_loop(0, CHUNKS, finish, 0)
+
+
+def finish_out(n, acc, lhs, rhs, out_ref, block, sems, tile_sems):
+    r = lax.axis_index("row")
+    feats = acc.shape[0]
+    width = acc.shape[1] // CHUNKS
+    ready = CHUNKS - TAIL
+
+    def columns(ch):
+        return pl.ds(ch * width, width)
+
+    for ch in range(ready):
+        pltpu.make_async_copy(acc.at[:, columns(ch)], out_ref.at[:, columns(ch)], sems.at[ch]).start()
+
+    for k in range(TAIL):
+        ch = ready + k
+
+        def tile_copy(i):
+            at = pl.ds(pl.multiple_of(i * TILE, TILE), TILE)
+            return pltpu.make_async_copy(
+                block.at[k, at, :], out_ref.at[at, columns(ch)], tile_sems.at[k, i]
+            )
+
+        def tile(i, carry):
+            at = pl.ds(pl.multiple_of(i * TILE, TILE), TILE)
+            at_end = (r == 0) | (r == n - 1)
+
+            @pl.when(at_end)
+            def _():
+                block[k, at, :] = acc[at, columns(ch)] + jnp.dot(
+                    lhs[at, :], rhs[k], preferred_element_type=jnp.float32
+                )
+
+            @pl.when(jnp.logical_not(at_end))
+            def _():
+                block[k, at, :] = acc[at, columns(ch)]
+
+            tile_copy(i).start()
+            return carry
+
+        lax.fori_loop(0, feats // TILE, tile, 0)
+
+    for ch in range(ready):
+        pltpu.make_async_copy(acc.at[:, columns(ch)], out_ref.at[:, columns(ch)], sems.at[ch]).wait()
+    for k in range(TAIL):
+        ch = ready + k
+
+        def tile_wait(i, carry):
+            at = pl.ds(pl.multiple_of(i * TILE, TILE), TILE)
+            pltpu.make_async_copy(
+                block.at[k, at, :], out_ref.at[at, columns(ch)], tile_sems.at[k, i]
+            ).wait()
+            return carry
+
+        lax.fori_loop(0, feats // TILE, tile_wait, 0)
 
 
 def fused(n, grads_now, grads_later):
     rows, feats = grads_now.shape
     cols = grads_later.shape[1]
-    return pl.pallas_call(
+    parts = pl.pallas_call(
         functools.partial(kernel, n),
-        out_shape=jax.ShapeDtypeStruct((feats, cols), jnp.float32),
+        out_shape=(
+            pltpu.VMEM((feats, cols), jnp.float32),
+            pltpu.VMEM((feats, 3 * rows), jnp.bfloat16),
+            pltpu.VMEM((TAIL, 3 * rows, cols // CHUNKS), jnp.bfloat16),
+        ),
         in_specs=[pl.BlockSpec(memory_space=pl.ANY)] * 2,
-        out_specs=pl.BlockSpec(memory_space=pl.ANY),
+        out_specs=(pl.BlockSpec(memory_space=pltpu.VMEM),) * 3,
         scratch_shapes=[
-            pltpu.VMEM((feats, cols), jnp.float32),
             pltpu.VMEM((4, feats, 3 * rows), jnp.bfloat16),
             pltpu.VMEM((3 * rows, cols // CHUNKS), jnp.bfloat16),
             pltpu.VMEM((n, CHUNKS, rows, cols // CHUNKS), jnp.float32),
@@ -245,10 +313,9 @@
             pltpu.SemaphoreType.DMA((3, CHUNKS)),
             pltpu.SemaphoreType.DMA((2, n, CHUNKS)),
             pltpu.SemaphoreType.DMA((n, CHUNKS)),
-            pltpu.SemaphoreType.DMA((CHUNKS,)),
         ],
         compiler_params=pltpu.CompilerParams(
-            collective_id=0, has_side_effects=True, vmem_limit_bytes=58 * 2**20
+            collective_id=0, has_side_effects=True, vmem_limit_bytes=FIRST_MIB * 2**20
         ),
         cost_estimate=pl.CostEstimate(
             flops=6 * n * rows * feats * cols,
@@ -256,6 +323,19 @@
             transcendentals=0,
         ),
     )(grads_now, grads_later)
+    parts = [pltpu.with_memory_space_constraint(part, pltpu.VMEM) for part in parts]
+    return pl.pallas_call(
+        functools.partial(finish_out, n),
+        out_shape=jax.ShapeDtypeStruct((feats, cols), jnp.float32),
+        in_specs=[pl.BlockSpec(memory_space=pltpu.VMEM)] * 3,
+        out_specs=pl.BlockSpec(memory_space=pl.ANY),
+        scratch_shapes=[
+            pltpu.VMEM((TAIL, feats, cols // CHUNKS), jnp.float32),
+            pltpu.SemaphoreType.DMA((CHUNKS,)),
+            pltpu.SemaphoreType.DMA((TAIL, feats // TILE)),
+        ],
+        compiler_params=pltpu.CompilerParams(vmem_limit_bytes=LAST_MIB * 2**20),
+    )(*parts)
 
 
 def gathered(grads_now, grads_later):
@@ -274,7 +354,7 @@
         shape["col"] == 4
         and n == 4
         and grads_later.shape[0] == rows
-        and rows % (32 * CHUNKS) == 0
+        and rows % (8 * CHUNKS) == 0
         and feats % TILE == 0
         and cols % (128 * CHUNKS) == 0
         and 4 * rows <= feats

time: 226 us -> 214 us (0.947)
  local copies, waits for them, and re-layouts: 11.8 us -> 0 us
    unnamed x1 -> x0, local copies, waits for them, and re-layouts: 11.8 us -> none
    pallas_call x1 -> x2, Pallas kernels: 214 us -> 214 us  [the longest x1 208 us: fused(): pl.pallas_call(functools.partial(kernel, n), out_shape=(pltpu.VMEM((feats...]
where the time goes in v2:
time: 214 us
  Pallas kernels  214 us (100%)
    pallas_call x1, Pallas kernels, fused(): pl.pallas_call(functools.partial(kernel, n), out_shape=(pltpu.VMEM((feats...  208 us
    pallas_call x1, Pallas kernels, fused(): pl.pallas_call(functools.partial(finish_out, n), out_shape=jax.ShapeDtype...  5.91 us

profile of v2, /device:TPU:0, one launch (start us, length us, event | category | flops | bytes accessed | tf_op | source)
XLA Modules:
  0.0 214.3 jit_solution(1432392749871311346)
XLA Ops:
  0.0 208.4 %shard_map.28 = (f32[2048,2048]{1,0:T(8,128)S(1)}, bf16[2048,1152]{1,0:T(8,128)(2,1)S(1)}, bf16[1,1152,512]{2,1,0:T(8,128)(2,1)S(1)}) custom-call(f32[384,2048]{1,0:T(8,128)} %now_ref.1, f32[384,2048]{1,0:T(8,128)} %later_ref.1), custom_call_target="tpu_custom_call" | custom-call | flops 38654705664 | bytes 41943040 | tf_op jit(solution)/shard_map/pallas_call | solution.py:297
  208.4 5.9 %shard_map.29 = f32[2048,2048]{1,0:T(8,128)} custom-call(f32[2048,2048]{1,0:T(8,128)S(1)} %get-tuple-element.8.acc, bf16[2048,1152]{1,0:T(8,128)(2,1)S(1)} %get-tuple-element.9.lhs, bf16[1,1152,512]{2,1,0:T(8,128)(2,1)S(1)} %get-tuple-element.10.rhs), custom_call_target="tpu_custom_call" | custom-call | tf_op jit(solution)/shard_map/pallas_call | solution.py:327

commit v3 on v2

--- a/solution.py
+++ b/solution.py
@@ -9,6 +9,7 @@
 
 MESH = pl.DeviceIdType.MESH
 CHUNKS = 4
+HALF = CHUNKS // 2
 FIRST_MIB = 34
 LAST_MIB = 10
 TAIL = 1
@@ -93,13 +94,15 @@
 
     pl.semaphore_wait(barrier, 2 + (r > 0).astype(jnp.int32) + (r < n - 1).astype(jnp.int32))
 
+    def own_line(side, ch):
+        return line_copy(side, r, ch, later_ref.at[:, columns(ch)], r - 1 + 2 * side)
+
     def start_own(ch, carry):
         for side in range(2):
-            target = r - 1 + 2 * side
-
-            @pl.when(in_line(target))
-            def _():
-                line_copy(side, r, ch, later_ref.at[:, columns(ch)], target).start()
+
+            @pl.when(in_line(r - 1 + 2 * side) & (ch < HALF))
+            def _():
+                own_line(side, ch).start()
 
         now_copy(1, ch, own_piece(ch), c, across).start()
         now_copy(0, ch, own_piece(ch), c, partner).start()
@@ -124,13 +127,25 @@
                 line_copy(side, origin, ch, held.at[origin, ch], target).start()
 
     def first(ch, carry):
+        for side in range(2):
+
+            @pl.when(in_line(r - 1 + 2 * side) & (ch < HALF))
+            def _():
+                own_line(side, ch).wait_send()
+                own_line(side, ch + HALF).start()
+
+        relay(1, ch, 0)
+        relay(1, ch, 1)
+        return carry
+
+    lax.fori_loop(0, CHUNKS, first, 0)
+
+    def cross(ch, carry):
         now_copy(1, ch, own_piece(ch), across, across).wait_recv()
         now_copy(2, ch, slot(across, ch), across, partner).start()
-        relay(1, ch, 0)
-        relay(1, ch, 1)
-        return carry
-
-    lax.fori_loop(0, CHUNKS, first, 0)
+        return carry
+
+    lax.fori_loop(0, CHUNKS, cross, 0)
 
     def settle(ch, carry):
         now_copy(0, ch, own_piece(ch), partner, partner).wait_recv()
@@ -227,7 +242,7 @@
             for d in range(n):
                 origin = r + d * (1 - 2 * side)
 
-                @pl.when(in_line(origin) & in_line(target))
+                @pl.when(in_line(origin) & in_line(target) & (d * CHUNKS + ch >= HALF))
                 def _():
                     line_copy(side, origin, ch, held.at[origin, ch], target).wait_send()
 

time: 214 us -> 233 us (1.089)
  Pallas kernels: 214 us -> 233 us
    pallas_call x1, Pallas kernels: 208 us -> 227 us  [fused(): pl.pallas_call(functools.partial(kernel, n), out_shape=(pltpu.VMEM((feats...]
where the time goes in v3:
time: 233 us
  Pallas kernels  233 us (100%)
    pallas_call x1, Pallas kernels, fused(): pl.pallas_call(functools.partial(kernel, n), out_shape=(pltpu.VMEM((feats...  227 us
    pallas_call x1, Pallas kernels, fused(): pl.pallas_call(functools.partial(finish_out, n), out_shape=jax.ShapeDtype...  5.91 us

profile of v3, /device:TPU:0, one launch (start us, length us, event | category | flops | bytes accessed | tf_op | source)
XLA Modules:
  0.0 232.8 jit_solution(9698127493095179180)
XLA Ops:
  0.0 226.9 %shard_map.28 = (f32[2048,2048]{1,0:T(8,128)S(1)}, bf16[2048,1152]{1,0:T(8,128)(2,1)S(1)}, bf16[1,1152,512]{2,1,0:T(8,128)(2,1)S(1)}) custom-call(f32[384,2048]{1,0:T(8,128)} %now_ref.1, f32[384,2048]{1,0:T(8,128)} %later_ref.1), custom_call_target="tpu_custom_call" | custom-call | flops 38654705664 | bytes 41943040 | tf_op jit(solution)/shard_map/pallas_call | solution.py:312
  226.9 5.9 %shard_map.29 = f32[2048,2048]{1,0:T(8,128)} custom-call(f32[2048,2048]{1,0:T(8,128)S(1)} %get-tuple-element.8.acc, bf16[2048,1152]{1,0:T(8,128)(2,1)S(1)} %get-tuple-element.9.lhs, bf16[1,1152,512]{2,1,0:T(8,128)(2,1)S(1)} %get-tuple-element.10.rhs), custom_call_target="tpu_custom_call" | custom-call | tf_op jit(solution)/shard_map/pallas_call | solution.py:342
